TPU v7x, 32 devices: a whole 2x2x4 slice. The times are simulated.
32 devices in a mesh: freq: 2 (over x), row: 4 (over y, core), col: 4 (over z).
Axes of the slice: x: 2, y: 2, z: 4, core: 2. Of those that a mesh axis runs over, the one named last changes fastest.
Arguments:
- b_stored: bfloat16 [1536, 6144], P('row', 'col'), may hold values from -0.5 to 0.5
- block_order: int32 [12], replicated, may hold values from 0 to 11, as said below
- pattern: int32 [12, 24], replicated, may hold values from 0 to 1, as said below
- eps_occ: float32 [2], replicated, may hold values from -1 to -0.3
- eps_vir: float32 [3072], replicated, may hold values from 0.1 to 3
- omega: float32 [2], P('freq'), parts along dimension 0, may hold values from 0.2 to 2
Outputs:
- chi_zero: float32 [3072, 1536], P(('freq', 'row'), 'col'), parts along dimension 0
There are 2 independent parts, one for each index of `freq`. A program takes and returns all parts, laid end to end along the dimension named above; an argument that names none is the same for every part. Nothing has to cross between parts.
Inputs may be any that keep to these rules, and one draw needn't show every extreme that they name: `block_order`: each auxiliary block stands in exactly one storage slot. For every pair tile t and every group of storage slots g * 3 to g * 3 + 2, exactly 2 of the blocks block_order[s] held in those slots have pattern 1 at tile t.
All inputs are finite; a program needn't handle non-finite values.
Results may differ from a plain program's by a relative error of at most 0.0013.
Values may be sent and summed in bfloat16 or wider, within the bound.
A program may use at most 64 MiB of HBM per device.

v0:
```python
import jax
import jax.numpy as jnp
from jax import lax
from jax.sharding import PartitionSpec as P

BLK = 128
BPR = 3
NV = 3072
TI = 256


def shards(b_stored, block_order, pattern, eps_occ, eps_vir, omega):
    pair_count = b_stored.shape[1]
    offset = lax.axis_index("col") * pair_count
    occ_index = offset // NV
    vir_first = offset % NV
    spacing = lax.dynamic_slice_in_dim(
        eps_vir, vir_first, pair_count, 0
    ) - lax.dynamic_slice_in_dim(eps_occ, occ_index, 1, 0)
    weight = 2.0 * spacing / (spacing * spacing + omega[0] * omega[0])
    tile_count = pair_count // TI
    tile_mask = lax.dynamic_slice_in_dim(pattern, offset // TI, tile_count, 1)
    screen = jnp.repeat(tile_mask, TI, axis=1).astype(jnp.bfloat16)
    gathered = lax.all_gather(b_stored, "row", axis=0, tiled=True)
    block_total = gathered.shape[0] // BLK
    inverse = (
        jnp.zeros((block_total,), jnp.int32)
        .at[block_order]
        .set(jnp.arange(block_total, dtype=jnp.int32))
    )
    blocks = gathered.reshape(block_total, BLK, pair_count)[inverse]
    masked = blocks * screen[:, None, :]
    left = lax.dynamic_slice_in_dim(masked, lax.axis_index("row") * BPR, BPR, 0).reshape(
        BPR * BLK, pair_count
    )
    masked = masked.reshape(block_total * BLK, pair_count)
    right = (masked.astype(jnp.float32) * weight[None, :]).astype(jnp.bfloat16)
    summed = lax.psum_scatter(
        lax.dot_general(right, left, (((1,), (1,)), ((), ())), preferred_element_type=jnp.float32),
        "col",
        scatter_dimension=0,
        tiled=True,
    )
    return summed.T


def solution(mesh):
    placed = (P("row", "col"), P(), P(), P(), P(), P("freq"))
    return jax.shard_map(
        shards, mesh=mesh, in_specs=placed, out_specs=P(("freq", "row"), "col"), check_vma=False
    )
```

profile of v0, /device:TPU:0, one launch (start us, length us, event | category | flops | bytes accessed | tf_op | source)
XLA Modules:
  0.0 120.2 jit_solution(16946678126108941712)
XLA Ops:
  6.5 0.0 all-gather.2.cloned.1.call-start
  6.5 0.7 all-gather.2.cloned.1.call-update
  7.3 0.0 reduce-scatter.2.cloned.1.call-start
  8.0 0.8 dynamic-slice_convert_fusion
  8.8 0.1 broadcast_in_dim.13
  8.9 1.2 %dynamic_slice.14 = f32[1]{0:T(128)} dynamic-slice(f32[2]{0:T(128)} %param.9, s32[]{:T(128)S(6)} %select_n.39), dynamic_slice_sizes={1} | dynamic-slice | bytes 12 | tf_op jit(solution)/shard_map/dynamic_slice | solution.py:19
  10.1 0.7 compare_select_fusion.1
  10.8 0.6 scatter_custom_fusion
  11.4 1.4 %add_divide_fusion = f32[1536]{0:T(1024)S(1)} fusion(f32[3072]{0:T(1024)} %param.10, s32[]{:T(128)S(6)} %select_n.37, f32[]{:T(128)} %bitcast.2, f32[]{:T(128)} %bitcast.1), kind=kLoop, calls=%fused_computation.4 | loop fusion | flops 7680 | bytes 12300 | tf_op jit(solution)/shard_map/div | solution.py:20
  12.8 36.3 %all-gather.2.cloned.1.call-done = bf16[1536,1536]{1,0:T(8,128)(2,1)} async-done(((bf16[384,1536]{1,0:T(8,128)(2,1)}), bf16[1536,1536]{1,0:T(8,128)(2,1)}) %all-gather.2.cloned.1.call-update) | async-done | bytes 4718608 | tf_op jit(solution)/shard_map/all_gather | solution.py:24
  49.1 5.5 %gather_fusion = bf16[12,128,1536]{2,1,0:T(8,128)(2,1)} fusion(bf16[12,128,1536]{2,1,0:T(8,128)(2,1)} %bitcast.12, s32[1024]{0:T(1024)S(1)} %pad_clamp_fusion), kind=kCustom, calls=%fused_computation | custom fusion | bytes 9437232 | tf_op jit(solution)/shard_map/gather | solution.py:31
  54.6 4.1 %multiply_convert_fusion = (bf16[12,128,1536]{2,1,0:T(8,128)(2,1)S(1)}, bf16[12,128,1536]{2,1,0:T(8,128)(2,1)S(1)}) fusion(f32[1536]{0:T(1024)S(1)} %add_divide_fusion, bf16[12,128,1536]{2,1,0:T(8,128)(2,1)} %gather_fusion, bf16[12,1536]{1,0:T(8,128)(2,1)S(1)} %bitcast.17), kind=kLoop, calls=%fused_computation.2 | loop fusion | flops 9437184 | bytes 14198784 | tf_op jit(solution)/shard_map/convert_element_type | solution.py:37
  58.8 0.1 constant_dynamic-slice_fusion
  58.9 4.1 %fusion.2 = f32[1536,384]{1,0:T(8,128)} fusion(bf16[1536,1536]{1,0:T(8,128)(2,1)S(1)} %bitcast.13, bf16[384,1536]{1,0:T(8,128)(2,1)S(1)} %bitcast.14), kind=kOutput, calls=%fused_computation.12 | convolution fusion | flops 1811939328 | bytes 8257536 | tf_op jit(solution)/shard_map/dot_general | solution.py:39
  63.0 0.0 reduce-scatter.2.cloned.1.call-update
  63.0 48.2 %reduce-scatter.2.cloned.1.call-done = f32[384,384]{1,0:T(8,128)} async-done(((f32[1536,384]{1,0:T(8,128)}), f32[384,384]{1,0:T(8,128)}) %reduce-scatter.2.cloned.1.call-update) | async-done | bytes 589840 | tf_op jit(solution)/shard_map/reduce_scatter | solution.py:38
  111.2 2.1 %copy.7 = f32[384,384]{1,0:T(8,128)} copy(f32[384,384]{0,1:T(8,128)} %bitcast.15) | data formatting | bytes 1179648 | tf_op jit(solution)/shard_map/transpose | solution.py:44
  (5 shorter events, 0.0 us)
Async XLA Ops:
  6.5 42.6 %all-gather.2.cloned.1.call-start = ((), (), s32[]{:S(2)}) async-start(), calls=%async_computation.1 | async-start | bytes 5898240 | tf_op jit(solution)/shard_map/all_gather | solution.py:24
  7.3 103.9 %reduce-scatter.2.cloned.1.call-start = ((), (), s32[]{:S(2)}) async-start(), calls=%async_computation.2 | async-start | bytes 2949120 | tf_op jit(solution)/shard_map/reduce_scatter | solution.py:38
Sparse Core Ops, SparseCore 0:
  8.9 40.1 all-gather.1
  63.1 48.0 reduce-scatter.1
where the time goes:
time: 121 us; the launch traced here: 120 us
  waiting for transfers between devices  85.2 us (70%)
  between operations  14.2 us (12%)
  local copies, waits for them, and re-layouts  9.66 us (8%)
  other arithmetic  6.92 us (6%)
  matrix products  4.12 us (3%)
    reduce_scatter x1, waiting for transfers between devices, shards(): lax.psum_scatter(lax.dot_general(right, left, (((1,), (1,)), ((), ())), p...  48.2 us
    all_gather x1, waiting for transfers between devices, shards(): gathered = lax.all_gather(b_stored, 'row', axis=0, tiled=True)  36.3 us
    gather x1, local copies, waits for them, and re-layouts, shards(): blocks = gathered.reshape(block_total, BLK, pair_count)[inverse]  5.51 us
    convert_element_type x1, other arithmetic, shards(): right = (masked.astype(jnp.float32) * weight[None, :]).astype(jnp.bfloat16)  4.12 us
    dot_general x1, matrix products, shards(): lax.dot_general(right, left, (((1,), (1,)), ((), ())), preferred_element_...  4.12 us
  transfers between devices with their start and end apart: 2, of which 2 were waited for; matrix products, arithmetic and copies ran while one was open for 4% of the time, Pallas kernels for 0%

commit v1 on v0

v1 whole, which is shorter than its diff:
```python
import functools
import jax
import jax.numpy as jnp
from jax import lax
from jax.experimental import pallas as pl
from jax.experimental.pallas import tpu as pltpu
from jax.sharding import PartitionSpec as P

BLK = 128
BPR = 3
LIVE = 2
NV = 3072
TI = 256
MESH = pl.DeviceIdType.MESH


def kernel(geo, order, pattern, occ, omega, vir, b_hbm, out, *scratch):
    rows, cols, chunks, tiles = geo
    wide = tiles * TI
    pairs = chunks * wide
    blocks = rows * BPR
    chips = rows // 2
    own_cols = blocks * BLK // cols
    stage, gath = scratch[:chunks], scratch[chunks : 2 * chunks]
    (inv, weight, left, right, sent, landed, in_sem, core_s, core_r, y_s, y_r, x_s, x_r,
     yc_s, yc_r, xc_s, xc_r, z_s, z_r) = scratch[2 * chunks :]
    x, r, z = lax.axis_index("freq"), lax.axis_index("row"), lax.axis_index("col")
    y = r // 2
    core = r - 2 * y
    mate = 2 * y + 1 - core

    loads = [
        pltpu.make_async_copy(b_hbm.at[:, :, pl.ds(j * wide, wide)], stage[j], in_sem.at[j])
        for j in range(chunks)
    ]
    for load in loads:
        load.start()

    barrier = pltpu.get_barrier_semaphore()

    def greet(where):
        pl.semaphore_signal(barrier, inc=1, device_id=where, device_id_type=MESH)

    greet({"row": mate})
    greet({"freq": 1 - x})
    for m in range(1, chips):
        greet({"row": 2 * lax.rem(y + m, chips) + core})
    for m in range(1, cols):
        greet({"col": z ^ m})

    def far(m, back):
        return 2 * lax.rem(y + (chips - m if back else m), chips) + core

    def remote(ref, send, recv, where):
        return pltpu.make_async_remote_copy(
            src_ref=ref, dst_ref=ref, send_sem=send, recv_sem=recv, device_id=where, device_id_type=MESH
        )

    def to_core(j, g):
        return remote(gath[j].at[pl.ds(LIVE * g, LIVE)], core_s.at[j], core_r.at[j], {"row": mate})

    def to_y(j, m, g, where):
        return remote(gath[j].at[LIVE * g + x], y_s.at[j, m - 1], y_r.at[j, m - 1], {"row": where})

    def to_x(j, m, g, half):
        return remote(gath[j].at[LIVE * g + half], x_s.at[j, m - 1], x_r.at[j, m - 1], {"freq": 1 - x})

    def y_core(j, m, g):
        return remote(gath[j].at[LIVE * g + x], yc_s.at[j, m - 1], yc_r.at[j, m - 1], {"row": mate})

    def x_core(j, m, g):
        return remote(gath[j].at[LIVE * g + 1 - x], xc_s.at[j, m - 1], xc_r.at[j, m - 1], {"row": mate})

    first_tile = z * (chunks * tiles)
    for j in range(chunks):
        loads[j].wait()
        for t in range(tiles):
            tile = first_tile + j * tiles + t
            span = pl.ds(t * TI, TI)
            low = pattern[order[BPR * r], tile]
            high = pattern[order[BPR * r + 2], tile]
            gath[j][LIVE * r, :, span] = stage[j][1 - low, :, span]
            gath[j][LIVE * r + 1, :, span] = stage[j][1 + high, :, span]
        if j == 0:
            pl.semaphore_wait(barrier, 2 + (chips - 1) + (cols - 1))
        for m in range(1, chips):
            to_y(j, m, r, far(m, False)).start()
        to_core(j, r).start()

    @pl.loop(0, blocks)
    def _(q):
        slot = jnp.int32(0)
        for s in range(blocks):
            slot = jnp.where(order[s] == q, s, slot)
        inv[q] = slot

    offset = z * pairs
    occ_index = offset // NV
    vir_first = pl.multiple_of(offset - occ_index * NV, TI)
    spacing = vir[:, pl.ds(vir_first, pairs)] - occ[occ_index]
    weight[...] = 2.0 * spacing / (spacing * spacing + omega[0] * omega[0])

    for j in range(chunks):
        for m in range(1, chips):
            g = far(m, True)
            to_y(j, m, g, r ^ 1).wait_recv()
            to_x(j, m, g, x).start()
            y_core(j, m, g).start()

    for j in range(chunks):
        for m in range(1, chips):
            g = far(m, True)
            to_x(j, m, g, 1 - x).wait_recv()
            x_core(j, m, g).start()
        to_core(j, mate).wait_recv()
        for m in range(1, chips):
            g = 2 * (far(m, True) // 2) + 1 - core
            y_core(j, m, g).wait_recv()
            x_core(j, m, g).wait_recv()

        def place(q, t):
            tile = first_tile + j * tiles + t
            slot = inv[q]
            group = slot // BPR
            at = slot - BPR * group
            low = pattern[order[BPR * group], tile]
            k = jnp.where(at == 2, 1, jnp.where(at == 1, low, 0))
            return gath[j][LIVE * group + k, :, t * TI : (t + 1) * TI], pattern[q, tile].astype(jnp.float32)

        @pl.loop(0, blocks)
        def _(q):
            for t in range(tiles):
                span = pl.ds(j * wide + t * TI, TI)
                value, live = place(q, t)
                right[pl.ds(pl.multiple_of(q * BLK, BLK), BLK), span] = (
                    value.astype(jnp.float32) * (weight[:, span] * live)
                ).astype(jnp.bfloat16)

        @pl.loop(0, BPR)
        def _(i):
            for t in range(tiles):
                span = pl.ds(j * wide + t * TI, TI)
                value, live = place(BPR * r + i, t)
                left[pl.ds(pl.multiple_of(i * BLK, BLK), BLK), span] = (
                    value.astype(jnp.float32) * live
                ).astype(jnp.bfloat16)

    def share(c):
        return lax.dot_general(
            left[...],
            right[pl.ds(pl.multiple_of(c * own_cols, BLK), own_cols), :],
            (((1,), (1,)), ((), ())),
            preferred_element_type=jnp.float32,
        )

    def to_z(m):
        return pltpu.make_async_remote_copy(
            src_ref=sent.at[m - 1], dst_ref=landed.at[m - 1], send_sem=z_s.at[m - 1], recv_sem=z_r.at[m - 1],
            device_id={"col": z ^ m}, device_id_type=MESH,
        )

    for m in range(cols - 1, 0, -1):
        sent[m - 1] = share(z ^ m).astype(jnp.bfloat16)
        to_z(m).start()
    out[...] = share(z)
    for m in range(cols - 1, 0, -1):
        to_z(m).wait_recv()
        out[...] += landed[m - 1].astype(jnp.float32)

    for m in range(1, cols):
        to_z(m).wait_send()
    for j in range(chunks):
        to_core(j, r).wait_send()
        for m in range(1, chips):
            g = far(m, True)
            to_y(j, m, r, far(m, False)).wait_send()
            to_x(j, m, g, x).wait_send()
            y_core(j, m, g).wait_send()
            x_core(j, m, g).wait_send()


def shards(rows, cols, b_stored, block_order, pattern, eps_occ, eps_vir, omega):
    pairs = b_stored.shape[1]
    count = pairs // TI
    tiles = 2 if count % 2 == 0 else 1
    chunks = count // tiles
    wide = tiles * TI
    chips = rows // 2
    height = b_stored.shape[0]
    own_cols = rows * height // cols
    dma = pltpu.SemaphoreType.DMA
    hop = dma((chunks, max(chips - 1, 1)))
    smem = pl.BlockSpec(memory_space=pltpu.SMEM)
    vmem = pl.BlockSpec(memory_space=pltpu.VMEM)
    return pl.pallas_call(
        functools.partial(kernel, (rows, cols, chunks, tiles)),
        out_shape=jax.ShapeDtypeStruct((height, own_cols), jnp.float32),
        in_specs=[smem, smem, smem, smem, vmem, pl.BlockSpec(memory_space=pl.ANY)],
        out_specs=vmem,
        scratch_shapes=[pltpu.VMEM((BPR, BLK, wide), jnp.bfloat16) for _ in range(chunks)]
        + [pltpu.VMEM((LIVE * rows, BLK, wide), jnp.bfloat16) for _ in range(chunks)]
        + [
            pltpu.SMEM((rows * BPR,), jnp.int32),
            pltpu.VMEM((1, pairs), jnp.float32),
            pltpu.VMEM((height, pairs), jnp.bfloat16),
            pltpu.VMEM((rows * height, pairs), jnp.bfloat16),
            pltpu.VMEM((cols - 1, height, own_cols), jnp.bfloat16),
            pltpu.VMEM((cols - 1, height, own_cols), jnp.bfloat16),
            dma((chunks,)),
            dma((chunks,)),
            dma((chunks,)),
            hop, hop, hop, hop, hop, hop, hop, hop,
            dma((cols - 1,)),
            dma((cols - 1,)),
        ],
        compiler_params=pltpu.CompilerParams(
            collective_id=0, has_side_effects=True, vmem_limit_bytes=56 * 2**20
        ),
        cost_estimate=pl.CostEstimate(
            flops=2 * height * rows * height * pairs, bytes_accessed=4 * height * pairs, transcendentals=0
        ),
    )(block_order, pattern, eps_occ, omega, eps_vir.reshape(1, -1), b_stored.reshape(BPR, BLK, pairs))


def solution(mesh):
    placed = (P("row", "col"), P(), P(), P(), P(), P("freq"))
    return jax.shard_map(
        functools.partial(shards, mesh.shape["row"], mesh.shape["col"]),
        mesh=mesh,
        in_specs=placed,
        out_specs=P(("freq", "row"), "col"),
        check_vma=False,
    )
```

time: 121 us -> 55.4 us (0.46)
  waiting for transfers between devices: 85.2 us -> 0 us
  Pallas kernels: 0 us -> 52.6 us
  between operations: 14.2 us -> 0.66 us
  local copies, waits for them, and re-layouts: 9.66 us -> 1.92 us
  other arithmetic: 6.92 us -> 0 us
  matrix products: 4.12 us -> 0 us
    pallas_call x0 -> x1, Pallas kernels: none -> 52.6 us  [shards(): pl.pallas_call(functools.partial(kernel, (rows, cols, chunks, tiles)), ou...]
    reduce_scatter x1 -> x0, waiting for transfers between devices: 48.2 us -> none  [shards(): lax.psum_scatter(lax.dot_general(right, left, (((1,), (1,)), ((), ())), p...]
    all_gather x1 -> x0, waiting for transfers between devices: 36.3 us -> none  [shards(): gathered = lax.all_gather(b_stored, 'row', axis=0, tiled=True)]
    gather x1 -> x0, local copies, waits for them, and re-layouts: 5.51 us -> none  [shards(): blocks = gathered.reshape(block_total, BLK, pair_count)[inverse]]
    convert_element_type x2 -> x0, other arithmetic: 4.9 us -> none  [the longest x1 4.12 us: shards(): right = (masked.astype(jnp.float32) * weight[None, :]).astype(jnp.bfloat16)]
    dot_general x1 -> x0, matrix products: 4.12 us -> none  [shards(): lax.dot_general(right, left, (((1,), (1,)), ((), ())), preferred_element_...]
    transpose x1 -> x0, local copies, waits for them, and re-layouts: 2.11 us -> none  [shards(): return summed.T]
    unnamed x2 -> x1, local copies, waits for them, and re-layouts: 0.03 us -> 1.92 us
  transfers between devices with their start and end apart: 2 -> 0, of which waited for: 2 -> 0; matrix products, arithmetic and copies ran while one was open for 4% -> 0% of each run, Pallas kernels for 0% -> 0%
where the time goes in v1:
time: 55.4 us; the launch traced here: 55.2 us
  Pallas kernels  52.6 us (95%)
  local copies, waits for them, and re-layouts  1.92 us (3%)
  between operations  0.66 us (1%)
    pallas_call x1, Pallas kernels, shards(): pl.pallas_call(functools.partial(kernel, (rows, cols, chunks, tiles)), ou...  52.6 us
    unnamed x1, local copies, waits for them, and re-layouts  1.92 us

profile of v1, /device:TPU:0, one launch (start us, length us, event | category | flops | bytes accessed | tf_op | source)
XLA Modules:
  0.0 55.2 jit_solution(17837513999696857528)
XLA Ops:
  0.7 52.6 %shard_map.64 = f32[384,384]{1,0:T(8,128)} custom-call(s32[12]{0:T(128)} %order.1, s32[12,24]{1,0:T(8,128)} %pattern.1, f32[2]{0:T(128)} %occ.1, f32[1]{0:T(128)S(6)} %copy.8.omega, f32[1,3072]{1,0:T(1,128)} %bitcast.3, bf16[3,128,1536]{2,1,0:T(8,128)(2,1)} %bitcast.2), custom_call_target="tpu_custom_call" | custom-call | flops 1811939328 | bytes 2359296 | tf_op jit(solution)/shard_map/pallas_call | solution.py:195
  53.3 1.9 %copy.9 = f32[384,384]{1,0:T(8,128)} copy(f32[384,384]{1,0:T(8,128)} %shard_map.64) | data formatting | bytes 1179648

commit v2 on v1

--- a/solution.py
+++ b/solution.py
@@ -182,7 +182,7 @@
 def shards(rows, cols, b_stored, block_order, pattern, eps_occ, eps_vir, omega):
     pairs = b_stored.shape[1]
     count = pairs // TI
-    tiles = 2 if count % 2 == 0 else 1
+    tiles = 1
     chunks = count // tiles
     wide = tiles * TI
     chips = rows // 2

time: 55.4 us -> 56.8 us (1.025)
  Pallas kernels: 52.6 us -> 54 us
    pallas_call x1, Pallas kernels: 52.6 us -> 54 us  [shards(): pl.pallas_call(functools.partial(kernel, (rows, cols, chunks, tiles)), ou...]
where the time goes in v2:
time: 56.8 us; the launch traced here: 56.6 us
  Pallas kernels  54 us (95%)
  local copies, waits for them, and re-layouts  1.92 us (3%)
  between operations  0.66 us (1%)
    pallas_call x1, Pallas kernels, shards(): pl.pallas_call(functools.partial(kernel, (rows, cols, chunks, tiles)), ou...  54 us
    unnamed x1, local copies, waits for them, and re-layouts  1.92 us

profile of v2, /device:TPU:0, one launch (start us, length us, event | category | flops | bytes accessed | tf_op | source)
XLA Modules:
  0.0 56.6 jit_solution(220098694573480111)
XLA Ops:
  0.7 54.0 %shard_map.64 = f32[384,384]{1,0:T(8,128)} custom-call(s32[12]{0:T(128)} %order.1, s32[12,24]{1,0:T(8,128)} %pattern.1, f32[2]{0:T(128)} %occ.1, f32[1]{0:T(128)S(6)} %copy.8.omega, f32[1,3072]{1,0:T(1,128)} %bitcast.3, bf16[3,128,1536]{2,1,0:T(8,128)(2,1)} %bitcast.2), custom_call_target="tpu_custom_call" | custom-call | flops 1811939328 | bytes 2359296 | tf_op jit(solution)/shard_map/pallas_call | solution.py:195
  54.7 1.9 %copy.9 = f32[384,384]{1,0:T(8,128)} copy(f32[384,384]{1,0:T(8,128)} %shard_map.64) | data formatting | bytes 1179648

commit v3 on v1

--- a/solution.py
+++ b/solution.py
@@ -10,6 +10,7 @@
 BPR = 3
 LIVE = 2
 NV = 3072
+EXTRA = 16
 TI = 256
 MESH = pl.DeviceIdType.MESH
 
@@ -21,9 +22,10 @@
     blocks = rows * BPR
     chips = rows // 2
     own_cols = blocks * BLK // cols
+    height = BPR * BLK
     stage, gath = scratch[:chunks], scratch[chunks : 2 * chunks]
-    (inv, weight, left, right, sent, landed, in_sem, core_s, core_r, y_s, y_r, x_s, x_r,
-     yc_s, yc_r, xc_s, xc_r, z_s, z_r) = scratch[2 * chunks :]
+    (inv, weight, left, right, sent, landed, relay, in_sem, core_s, core_r, y_s, y_r, x_s, x_r,
+     yc_s, yc_r, xc_s, xc_r, z_s, z_r, relay_r) = scratch[2 * chunks :]
     x, r, z = lax.axis_index("freq"), lax.axis_index("row"), lax.axis_index("col")
     y = r // 2
     core = r - 2 * y
@@ -153,22 +155,78 @@
             preferred_element_type=jnp.float32,
         )
 
-    def to_z(m):
-        return pltpu.make_async_remote_copy(
-            src_ref=sent.at[m - 1], dst_ref=landed.at[m - 1], send_sem=z_s.at[m - 1], recv_sem=z_r.at[m - 1],
-            device_id={"col": z ^ m}, device_id_type=MESH,
-        )
-
-    for m in range(cols - 1, 0, -1):
-        sent[m - 1] = share(z ^ m).astype(jnp.bfloat16)
-        to_z(m).start()
+    pair = z // 2
+    odd = lax.rem(pair, 2)
+    inner = 2 * pair + 1 - odd
+    outer = 2 * pair + odd
+    relays = cols - 2
+
+    def target(i):
+        other = pair ^ (1 + i // 2)
+        return 2 * other + (lax.rem(other, 2) if i % 2 == 0 else 1 - lax.rem(other, 2))
+
+    def to_mate():
+        return pltpu.make_async_remote_copy(
+            src_ref=sent.at[relays], dst_ref=landed.at[0], send_sem=z_s.at[relays], recv_sem=z_r.at[0],
+            device_id={"col": z ^ 1}, device_id_type=MESH,
+        )
+
+    def to_relay(i):
+        return pltpu.make_async_remote_copy(
+            src_ref=sent.at[i], dst_ref=relay.at[i], send_sem=z_s.at[i], recv_sem=relay_r.at[i],
+            device_id={"col": z ^ 1}, device_id_type=MESH,
+        )
+
+    def to_target(i):
+        m = 1 + i // 2
+        return pltpu.make_async_remote_copy(
+            src_ref=sent.at[i], dst_ref=landed.at[m], send_sem=z_s.at[i], recv_sem=z_r.at[m],
+            device_id={"col": target(i)}, device_id_type=MESH,
+        )
+
+    gap = lax.broadcasted_iota(jnp.int32, (height, own_cols), 1) - lax.broadcasted_iota(
+        jnp.int32, (height, own_cols), 0
+    )
+
+    def pack(i, value, c):
+        rounded = value.astype(jnp.bfloat16)
+        sent[i, pl.ds(0, height), :] = rounded
+        rest = jnp.where(gap == r * height - c * own_cols, value - rounded.astype(jnp.float32), 0.0)
+        sent[i, pl.ds(height, EXTRA), :] = jnp.broadcast_to(
+            jnp.sum(rest, axis=0, keepdims=True), (EXTRA, own_cols)
+        ).astype(jnp.bfloat16)
+
+    def unpack(ref, i, c):
+        rest = ref[i, pl.ds(height, EXTRA), :].astype(jnp.float32)[0:1]
+        return ref[i, pl.ds(0, height), :].astype(jnp.float32) + jnp.where(
+            gap == r * height - c * own_cols, rest, 0.0
+        )
+
+    @pl.when(z == outer)
+    def _():
+        for i in range(relays):
+            pack(i, share(target(i)), target(i))
+            to_relay(i).start()
+        pack(relays, share(inner), inner)
+        to_mate().start()
+
+    @pl.when(z == inner)
+    def _():
+        pack(relays, share(outer), outer)
+        to_mate().start()
+        for i in range(relays):
+            out[...] = share(target(i))
+            to_relay(i).wait_recv()
+            pack(i, out[...] + unpack(relay, i, target(i)), target(i))
+            to_target(i).start()
+
     out[...] = share(z)
-    for m in range(cols - 1, 0, -1):
-        to_z(m).wait_recv()
-        out[...] += landed[m - 1].astype(jnp.float32)
-
-    for m in range(1, cols):
-        to_z(m).wait_send()
+    for m in range(cols // 2):
+        (to_mate() if m == 0 else to_target(2 * (m - 1))).wait_recv()
+        out[...] += unpack(landed, m, z)
+    to_mate().wait_send()
+    for i in range(relays):
+        to_relay(i).wait_send()
     for j in range(chunks):
         to_core(j, r).wait_send()
         for m in range(1, chips):
@@ -204,14 +262,16 @@
             pltpu.VMEM((1, pairs), jnp.float32),
             pltpu.VMEM((height, pairs), jnp.bfloat16),
             pltpu.VMEM((rows * height, pairs), jnp.bfloat16),
-            pltpu.VMEM((cols - 1, height, own_cols), jnp.bfloat16),
-            pltpu.VMEM((cols - 1, height, own_cols), jnp.bfloat16),
+            pltpu.VMEM((cols - 1, height + EXTRA, own_cols), jnp.bfloat16),
+            pltpu.VMEM((cols // 2, height + EXTRA, own_cols), jnp.bfloat16),
+            pltpu.VMEM((cols - 2, height + EXTRA, own_cols), jnp.bfloat16),
             dma((chunks,)),
             dma((chunks,)),
             dma((chunks,)),
             hop, hop, hop, hop, hop, hop, hop, hop,
             dma((cols - 1,)),
-            dma((cols - 1,)),
+            dma((cols // 2,)),
+            dma((cols - 2,)),
         ],
         compiler_params=pltpu.CompilerParams(
             collective_id=0, has_side_effects=True, vmem_limit_bytes=56 * 2**20

time: 55.4 us -> 49.5 us (0.89); the launches traced: 55.2 us -> 48.6 us
  Pallas kernels: 52.6 us -> 46.1 us
    pallas_call x1, Pallas kernels: 52.6 us -> 46.1 us  [shards(): pl.pallas_call(functools.partial(kernel, (rows, cols, chunks, tiles)), ou...]
where the time goes in v3:
time: 49.5 us; the launch traced here: 48.6 us
  Pallas kernels  46.1 us (93%)
  local copies, waits for them, and re-layouts  1.92 us (4%)
  between operations  0.66 us (1%)
    pallas_call x1, Pallas kernels, shards(): pl.pallas_call(functools.partial(kernel, (rows, cols, chunks, tiles)), ou...  46.1 us
    unnamed x1, local copies, waits for them, and re-layouts  1.92 us

profile of v3, /device:TPU:0, one launch (start us, length us, event | category | flops | bytes accessed | tf_op | source)
XLA Modules:
  0.0 48.6 jit_solution(2596157633391107049)
XLA Ops:
  0.7 46.1 %shard_map.64 = f32[384,384]{1,0:T(8,128)} custom-call(s32[12]{0:T(128)} %order.1, s32[12,24]{1,0:T(8,128)} %pattern.1, f32[2]{0:T(128)} %occ.1, f32[1]{0:T(128)S(6)} %copy.8.omega, f32[1,3072]{1,0:T(1,128)} %bitcast.3, bf16[3,128,1536]{2,1,0:T(8,128)(2,1)} %bitcast.2), custom_call_target="tpu_custom_call" | custom-call | flops 1811939328 | bytes 2359296 | tf_op jit(solution)/shard_map/pallas_call | solution.py:253
  46.7 1.9 %copy.9 = f32[384,384]{1,0:T(8,128)} copy(f32[384,384]{1,0:T(8,128)} %shard_map.64) | data formatting | bytes 1179648

commit v4 on v3

--- a/solution.py
+++ b/solution.py
@@ -58,17 +58,20 @@
             src_ref=ref, dst_ref=ref, send_sem=send, recv_sem=recv, device_id=where, device_id_type=MESH
         )
 
+    def part(j, g):
+        return gath[j].at[pl.ds(LIVE * g, LIVE)] if j == chunks - 1 else gath[j].at[LIVE * g + x]
+
     def to_core(j, g):
         return remote(gath[j].at[pl.ds(LIVE * g, LIVE)], core_s.at[j], core_r.at[j], {"row": mate})
 
     def to_y(j, m, g, where):
-        return remote(gath[j].at[LIVE * g + x], y_s.at[j, m - 1], y_r.at[j, m - 1], {"row": where})
+        return remote(part(j, g), y_s.at[j, m - 1], y_r.at[j, m - 1], {"row": where})
 
     def to_x(j, m, g, half):
         return remote(gath[j].at[LIVE * g + half], x_s.at[j, m - 1], x_r.at[j, m - 1], {"freq": 1 - x})
 
     def y_core(j, m, g):
-        return remote(gath[j].at[LIVE * g + x], yc_s.at[j, m - 1], yc_r.at[j, m - 1], {"row": mate})
+        return remote(part(j, g), yc_s.at[j, m - 1], yc_r.at[j, m - 1], {"row": mate})
 
     def x_core(j, m, g):
         return remote(gath[j].at[LIVE * g + 1 - x], xc_s.at[j, m - 1], xc_r.at[j, m - 1], {"row": mate})
@@ -106,19 +109,22 @@
         for m in range(1, chips):
             g = far(m, True)
             to_y(j, m, g, r ^ 1).wait_recv()
-            to_x(j, m, g, x).start()
+            if j < chunks - 1:
+                to_x(j, m, g, x).start()
             y_core(j, m, g).start()
 
     for j in range(chunks):
         for m in range(1, chips):
             g = far(m, True)
-            to_x(j, m, g, 1 - x).wait_recv()
-            x_core(j, m, g).start()
+            if j < chunks - 1:
+                to_x(j, m, g, 1 - x).wait_recv()
+                x_core(j, m, g).start()
         to_core(j, mate).wait_recv()
         for m in range(1, chips):
             g = 2 * (far(m, True) // 2) + 1 - core
             y_core(j, m, g).wait_recv()
-            x_core(j, m, g).wait_recv()
+            if j < chunks - 1:
+                x_core(j, m, g).wait_recv()
 
         def place(q, t):
             tile = first_tile + j * tiles + t
@@ -232,9 +238,10 @@
         for m in range(1, chips):
             g = far(m, True)
             to_y(j, m, r, far(m, False)).wait_send()
-            to_x(j, m, g, x).wait_send()
             y_core(j, m, g).wait_send()
-            x_core(j, m, g).wait_send()
+            if j < chunks - 1:
+                to_x(j, m, g, x).wait_send()
+                x_core(j, m, g).wait_send()
 
 
 def shards(rows, cols, b_stored, block_order, pattern, eps_occ, eps_vir, omega):

time: 49.5 us -> 48.3 us (0.976)
  Pallas kernels: 46.1 us -> 45.2 us
    pallas_call x1, Pallas kernels: 46.1 us -> 45.2 us  [shards(): pl.pallas_call(functools.partial(kernel, (rows, cols, chunks, tiles)), ou...]
where the time goes in v4:
time: 48.3 us; the launch traced here: 47.8 us
  Pallas kernels  45.2 us (94%)
  local copies, waits for them, and re-layouts  1.92 us (4%)
  between operations  0.66 us (1%)
    pallas_call x1, Pallas kernels, shards(): pl.pallas_call(functools.partial(kernel, (rows, cols, chunks, tiles)), ou...  45.2 us
    unnamed x1, local copies, waits for them, and re-layouts  1.92 us

profile of v4, /device:TPU:0, one launch (start us, length us, event | category | flops | bytes accessed | tf_op | source)
XLA Modules:
  0.0 47.8 jit_solution(437850269382764818)
XLA Ops:
  0.7 45.2 %shard_map.64 = f32[384,384]{1,0:T(8,128)} custom-call(s32[12]{0:T(128)} %order.1, s32[12,24]{1,0:T(8,128)} %pattern.1, f32[2]{0:T(128)} %occ.1, f32[1]{0:T(128)S(6)} %copy.8.omega, f32[1,3072]{1,0:T(1,128)} %bitcast.3, bf16[3,128,1536]{2,1,0:T(8,128)(2,1)} %bitcast.2), custom_call_target="tpu_custom_call" | custom-call | flops 1811939328 | bytes 2359296 | tf_op jit(solution)/shard_map/pallas_call | solution.py:260
  45.9 1.9 %copy.9 = f32[384,384]{1,0:T(8,128)} copy(f32[384,384]{1,0:T(8,128)} %shard_map.64) | data formatting | bytes 1179648

commit v5 on v4

--- a/solution.py
+++ b/solution.py
@@ -16,9 +16,10 @@
 
 
 def kernel(geo, order, pattern, occ, omega, vir, b_hbm, out, *scratch):
-    rows, cols, chunks, tiles = geo
-    wide = tiles * TI
-    pairs = chunks * wide
+    rows, cols, tiles = geo
+    chunks = len(tiles)
+    first = [sum(tiles[:j]) for j in range(chunks)]
+    pairs = sum(tiles) * TI
     blocks = rows * BPR
     chips = rows // 2
     own_cols = blocks * BLK // cols
@@ -32,7 +33,7 @@
     mate = 2 * y + 1 - core
 
     loads = [
-        pltpu.make_async_copy(b_hbm.at[:, :, pl.ds(j * wide, wide)], stage[j], in_sem.at[j])
+        pltpu.make_async_copy(b_hbm.at[:, :, pl.ds(first[j] * TI, tiles[j] * TI)], stage[j], in_sem.at[j])
         for j in range(chunks)
     ]
     for load in loads:
@@ -76,11 +77,11 @@
     def x_core(j, m, g):
         return remote(gath[j].at[LIVE * g + 1 - x], xc_s.at[j, m - 1], xc_r.at[j, m - 1], {"row": mate})
 
-    first_tile = z * (chunks * tiles)
+    first_tile = z * sum(tiles)
     for j in range(chunks):
         loads[j].wait()
-        for t in range(tiles):
-            tile = first_tile + j * tiles + t
+        for t in range(tiles[j]):
+            tile = first_tile + first[j] + t
             span = pl.ds(t * TI, TI)
             low = pattern[order[BPR * r], tile]
             high = pattern[order[BPR * r + 2], tile]
@@ -127,7 +128,7 @@
                 x_core(j, m, g).wait_recv()
 
         def place(q, t):
-            tile = first_tile + j * tiles + t
+            tile = first_tile + first[j] + t
             slot = inv[q]
             group = slot // BPR
             at = slot - BPR * group
@@ -137,8 +138,8 @@
 
         @pl.loop(0, blocks)
         def _(q):
-            for t in range(tiles):
-                span = pl.ds(j * wide + t * TI, TI)
+            for t in range(tiles[j]):
+                span = pl.ds((first[j] + t) * TI, TI)
                 value, live = place(q, t)
                 right[pl.ds(pl.multiple_of(q * BLK, BLK), BLK), span] = (
                     value.astype(jnp.float32) * (weight[:, span] * live)
@@ -146,8 +147,8 @@
 
         @pl.loop(0, BPR)
         def _(i):
-            for t in range(tiles):
-                span = pl.ds(j * wide + t * TI, TI)
+            for t in range(tiles[j]):
+                span = pl.ds((first[j] + t) * TI, TI)
                 value, live = place(BPR * r + i, t)
                 left[pl.ds(pl.multiple_of(i * BLK, BLK), BLK), span] = (
                     value.astype(jnp.float32) * live
@@ -247,9 +248,8 @@
 def shards(rows, cols, b_stored, block_order, pattern, eps_occ, eps_vir, omega):
     pairs = b_stored.shape[1]
     count = pairs // TI
-    tiles = 2 if count % 2 == 0 else 1
-    chunks = count // tiles
-    wide = tiles * TI
+    tiles = (2,) * (count // 2 - 1) + (1, 1) if count % 2 == 0 else (1,) * count
+    chunks = len(tiles)
     chips = rows // 2
     height = b_stored.shape[0]
     own_cols = rows * height // cols
@@ -258,12 +258,12 @@
     smem = pl.BlockSpec(memory_space=pltpu.SMEM)
     vmem = pl.BlockSpec(memory_space=pltpu.VMEM)
     return pl.pallas_call(
-        functools.partial(kernel, (rows, cols, chunks, tiles)),
+        functools.partial(kernel, (rows, cols, tiles)),
         out_shape=jax.ShapeDtypeStruct((height, own_cols), jnp.float32),
         in_specs=[smem, smem, smem, smem, vmem, pl.BlockSpec(memory_space=pl.ANY)],
         out_specs=vmem,
-        scratch_shapes=[pltpu.VMEM((BPR, BLK, wide), jnp.bfloat16) for _ in range(chunks)]
-        + [pltpu.VMEM((LIVE * rows, BLK, wide), jnp.bfloat16) for _ in range(chunks)]
+        scratch_shapes=[pltpu.VMEM((BPR, BLK, n * TI), jnp.bfloat16) for n in tiles]
+        + [pltpu.VMEM((LIVE * rows, BLK, n * TI), jnp.bfloat16) for n in tiles]
         + [
             pltpu.SMEM((rows * BPR,), jnp.int32),
             pltpu.VMEM((1, pairs), jnp.float32),

time: 48.3 us -> 50.4 us (1.043)
  the two profiles are of different devices: /device:TPU:0 before, /device:TPU:8 now
where the time goes in v5:
time: 50.4 us; the launch traced here: 50.2 us
  Pallas kernels  47.6 us (94%)
  local copies, waits for them, and re-layouts  1.92 us (4%)
  between operations  0.66 us (1%)
    pallas_call x1, Pallas kernels, shards(): pl.pallas_call(functools.partial(kernel, (rows, cols, tiles)), out_shape=...  47.6 us
    unnamed x1, local copies, waits for them, and re-layouts  1.92 us

profile of v5, /device:TPU:8, one launch (start us, length us, event | category | flops | bytes accessed | tf_op | source)
XLA Modules:
  0.0 50.2 jit_solution(5892839709778028739)
XLA Ops:
  0.7 47.6 %shard_map.64 = f32[384,384]{1,0:T(8,128)} custom-call(s32[12]{0:T(128)} %order.1, s32[12,24]{1,0:T(8,128)} %pattern.1, f32[2]{0:T(128)} %occ.1, f32[1]{0:T(128)S(6)} %copy.8.omega, f32[1,3072]{1,0:T(1,128)} %bitcast.3, bf16[3,128,1536]{2,1,0:T(8,128)(2,1)} %bitcast.2), custom_call_target="tpu_custom_call" | custom-call | flops 1811939328 | bytes 2359296 | tf_op jit(solution)/shard_map/pallas_call | solution.py:260
  48.3 1.9 %copy.9 = f32[384,384]{1,0:T(8,128)} copy(f32[384,384]{1,0:T(8,128)} %shard_map.64) | data formatting | bytes 1179648

commit v6 on v5

--- a/solution.py
+++ b/solution.py
@@ -248,7 +248,7 @@
 def shards(rows, cols, b_stored, block_order, pattern, eps_occ, eps_vir, omega):
     pairs = b_stored.shape[1]
     count = pairs // TI
-    tiles = (2,) * (count // 2 - 1) + (1, 1) if count % 2 == 0 else (1,) * count
+    tiles = (count // 2, count // 2 - 1, 1) if count % 2 == 0 and count > 2 else (1,) * count
     chunks = len(tiles)
     chips = rows // 2
     height = b_stored.shape[0]

time: 50.4 us -> 48.9 us (0.970)
  the two profiles are of different devices: /device:TPU:8 before, /device:TPU:0 now
where the time goes in v6:
time: 48.9 us; the launch traced here: 48.5 us
  Pallas kernels  46 us (94%)
  local copies, waits for them, and re-layouts  1.92 us (4%)
  between operations  0.66 us (1%)
    pallas_call x1, Pallas kernels, shards(): pl.pallas_call(functools.partial(kernel, (rows, cols, tiles)), out_shape=...  46 us
    unnamed x1, local copies, waits for them, and re-layouts  1.92 us

profile of v6, /device:TPU:0, one launch (start us, length us, event | category | flops | bytes accessed | tf_op | source)
XLA Modules:
  0.0 48.5 jit_solution(8098690788286281563)
XLA Ops:
  0.7 46.0 %shard_map.64 = f32[384,384]{1,0:T(8,128)} custom-call(s32[12]{0:T(128)} %order.1, s32[12,24]{1,0:T(8,128)} %pattern.1, f32[2]{0:T(128)} %occ.1, f32[1]{0:T(128)S(6)} %copy.8.omega, f32[1,3072]{1,0:T(1,128)} %bitcast.3, bf16[3,128,1536]{2,1,0:T(8,128)(2,1)} %bitcast.2), custom_call_target="tpu_custom_call" | custom-call | flops 1811939328 | bytes 2359296 | tf_op jit(solution)/shard_map/pallas_call | solution.py:260
  46.6 1.9 %copy.9 = f32[384,384]{1,0:T(8,128)} copy(f32[384,384]{1,0:T(8,128)} %shard_map.64) | data formatting | bytes 1179648
